TPU v7x, 512 devices: a whole 4x8x8 slice. The times are simulated.
512 devices in a mesh: vol: 32 (over x, z), nar: 16 (over y, core).
Axes of the slice: x: 4, y: 8, z: 8, core: 2. Of those that a mesh axis runs over, the one named last changes fastest.
Arguments:
- series: bfloat16 [32768, 2048], P(('vol', 'nar')), may hold values from -6 to 6
- send_rows: int32 [32, 16, 64], P('vol', 'nar'), may hold values from -1 to 63, as said below
- bin_counts: int32 [16], replicated, may hold values from 1 to 32, 256 in all
- observer_cells: int32 [2, 512], replicated, may hold values from 0 to 127
Outputs:
- spectra_out: float32 [16, 32, 2, 512], P('nar', 'vol')
Inputs may be any that keep to these rules, and one draw needn't show every extreme that they name: `send_rows`: entry (u, n, k) names the row of device (u, n)'s 64 rows of series for slot k mod 2 bound for the patch owner at vol index k // 2 and nar index n, or is -1 for an empty slot; one device never names a row twice. Nar index m owns bin_counts[m] bins in order, from the sum of the counts before m on; some owner holds exactly 32 bins. `observer_cells`: row 0 holds polar indices, row 1 azimuthal indices.
All inputs are finite; a program needn't handle non-finite values.
Results may differ from a plain program's by a relative error of at most 0.0043.
Values may be sent and summed in bfloat16 or wider, within the bound.
A program may use at most 64 MiB of HBM per device.

v0:
```python
import math

import jax
import jax.numpy as jnp
import ml_dtypes
import numpy as np
from jax import lax
from jax.experimental import pallas as pl
from jax.experimental.pallas import tpu as pltpu
from jax.sharding import PartitionSpec as P

NT = 512
NF = 256
NQ = 4
OBS = 512
WAVE_STEP = 0.05
BF = jnp.bfloat16
F32 = jnp.float32
MESH = pl.DeviceIdType.MESH


def dft_rows():
    steps = np.arange(NT, dtype=np.int64)
    turns = (np.arange(1, NF + 1, dtype=np.int64)[:, None] * steps[None, :]) % NT
    angle = turns.astype(np.float32) * np.float32(2.0 * math.pi / NT)
    table = np.stack([np.cos(angle), -np.sin(angle)], axis=1)
    return table.reshape(2 * NF, NT).astype(ml_dtypes.bfloat16)


SIN_TERMS = [(-1.0) ** i / math.factorial(2 * i + 1) for i in range(7)]
COS_TERMS = [(-1.0) ** i / math.factorial(2 * i) for i in range(8)]


def polynomial(terms, square):
    total = terms[-1]
    for term in terms[-2::-1]:
        total = total * square + term
    return total


def cos_sin(turns):
    half = (turns - jnp.round(turns)) * math.pi
    square = half * half
    s = half * polynomial(SIN_TERMS, square)
    c = polynomial(COS_TERMS, square)
    return 1.0 - 2.0 * s * s, 2.0 * s * c


def times(one, other):
    return one[0] * other[0] - one[1] * other[1], one[0] * other[1] + one[1] * other[0]


def squared(one):
    return 1.0 - 2.0 * one[1] * one[1], 2.0 * one[0] * one[1]


def modulo(value, base):
    rest = value - (value.astype(F32) * (1.0 / base)).astype(jnp.int32) * base
    rest = jnp.where(rest < 0, rest + base, rest)
    return jnp.where(rest >= base, rest - base, rest)


def kernel(
    counts_ref,
    series_ref,
    listing_ref,
    cells_ref,
    dft_ref,
    out_ref,
    spec,
    own,
    swap_out,
    swap_in,
    place,
    facing,
    weight,
    table,
    coef,
    stage,
    part_out,
    part_in,
    slot_out,
    slot_in,
    last_out,
    last_in,
    swap_sems,
    part_sems,
    slot_sems,
    last_sems,
):
    u = lax.axis_index("vol")
    n = lax.axis_index("nar")
    x, z = u // 8, u % 8
    core = n % 2
    vols, nars = 32, 16

    barrier = pltpu.get_barrier_semaphore()

    def greet_vol(k, carry):
        pl.semaphore_signal(barrier, inc=1, device_id={"vol": (u + k) % vols}, device_id_type=MESH)
        return carry

    def greet_nar(k, carry):
        pl.semaphore_signal(barrier, inc=1, device_id={"nar": (n + k) % nars}, device_id_type=MESH)
        return carry

    lax.fori_loop(1, vols, greet_vol, 0)
    lax.fori_loop(1, nars, greet_nar, 0)

    rows = jnp.concatenate([series_ref[:, q * NT : (q + 1) * NT] for q in range(NQ)], axis=0)
    spectra = lax.dot_general(
        dft_ref[...], rows, (((1,), (1,)), ((), ())), preferred_element_type=F32
    )
    spectra = (spectra * (1.0 / math.sqrt(NT))).astype(BF)
    listing = listing_ref[...]
    listing = jnp.concatenate([listing, listing], axis=1)
    slot = lax.broadcasted_iota(jnp.int32, (256, 128), 1)
    line = lax.broadcasted_iota(jnp.int32, (256, 128), 0)
    mine = (slot // 64 == core) & (line % 64 == listing)
    for q in range(NQ):
        pick = jnp.where(mine & (line // 64 == q), 1.0, 0.0).astype(BF)
        spec[pl.ds(q, 2 * NF, stride=NQ), :] = jnp.dot(spectra, pick, preferred_element_type=F32)
    swap_out[...] = spec[pl.ds(pl.multiple_of((1 - core) * 1024, 1024), 1024), :].astype(BF)

    pl.semaphore_wait(barrier, vols + nars - 2)
    swap = pltpu.make_async_remote_copy(
        src_ref=swap_out,
        dst_ref=swap_in,
        send_sem=swap_sems.at[0],
        recv_sem=swap_sems.at[1],
        device_id={"nar": n + 1 - 2 * core},
        device_id_type=MESH,
    )
    swap.start()

    slab = u * 8 + n // 2
    point = slab * 128 + lax.broadcasted_iota(jnp.int32, (128, 128), 0)
    c, s = cos_sin(modulo(point * 1597, 8191).astype(F32) * (1.0 / 8191.0))
    place[0] = 20.0 * c
    place[1] = 20.0 * s
    place[2] = slab.astype(F32) * 0.5 + modulo(point * 613, 127).astype(F32) * (0.37 / 127.0)
    cells = cells_ref[...].astype(F32)
    polar = cos_sin((cells[0:1] + 0.5) * (1.0 / 256.0))
    azimuth = cos_sin(cells[1:2] * (1.0 / 128.0))
    facing[0] = jnp.broadcast_to(polar[1] * azimuth[0], (8, OBS))
    facing[1] = jnp.broadcast_to(polar[1] * azimuth[1], (8, OBS))
    facing[2] = jnp.broadcast_to(polar[0], (8, OBS))
    term = lax.broadcasted_iota(jnp.int32, (8, OBS), 0) % NQ
    weight[...] = jnp.where(
        term == 0,
        1.0,
        jnp.where(term == 1, facing[0], jnp.where(term == 2, facing[1], facing[2])),
    )

    def fill(at, carry):
        rows16 = pl.ds(pl.multiple_of((at // 2) * 16, 16), 16)
        lanes = pl.ds(pl.multiple_of((at % 2) * 256, 256), 256)
        dotted = 0.0
        for axis in range(3):
            spot = place[axis, rows16, :]
            look = facing[axis, :, lanes]
            dotted = dotted + jnp.concatenate([spot, spot], axis=1) * jnp.concatenate([look, look], axis=0)
        turns = dotted * (WAVE_STEP / (2.0 * math.pi))

        def keep(index, value):
            table[index, rows16, lanes] = value[0].astype(BF)
            table[index + 1, rows16, lanes] = value[1].astype(BF)

        fine = cos_sin(turns * 0.5)
        step = squared(fine)
        keep(16, fine)
        for i in range(1, 8):
            fine = times(fine, step)
            keep(16 + 2 * i, fine)
        for _ in range(4):
            step = squared(step)
        coarse = cos_sin(turns * (core.astype(F32) * 128.0 + 8.5))
        keep(0, coarse)
        for g in range(1, 8):
            coarse = times(coarse, step)
            keep(2 * g, coarse)
        return carry

    lax.fori_loop(0, 16, fill, 0)

    swap.wait()
    base = core * 1024

    def join(at, carry):
        here = pl.multiple_of(at * 64, 64)
        own[pl.ds(here, 64), :] = (
            spec[pl.ds(pl.multiple_of(base + here, 64), 64), :] + swap_in[pl.ds(here, 64), :].astype(F32)
        )
        return carry

    lax.fori_loop(0, 16, join, 0)
    sign = jnp.where(lax.broadcasted_iota(jnp.int32, (8, 128), 0) < 4, 1.0, -1.0)

    def lay(g, carry):
        for i in range(8):
            high = own[pl.ds(pl.multiple_of((16 * g + 8 + i) * 8, 8), 8), :]
            low = own[pl.ds(pl.multiple_of((16 * g + 7 - i) * 8, 8), 8), :]
            high2 = pltpu.roll(high, 4, 0) * sign
            low2 = pltpu.roll(low, 4, 0) * sign
            blocks = ((high, low), (-high, low), (high2, low2), (high2, -low2))
            for k, both in enumerate(blocks):
                coef[i, g, :, pl.ds(k * 128, 128)] = jnp.concatenate(both, axis=0).astype(BF)
        return carry

    lax.fori_loop(0, 8, lay, 0)

    def one_fine(step, carry):
        i = (step + z) % 8
        for g in range(8):
            for half in range(2):
                lanes = pl.ds(half * 256, 256)
                c, s = table[2 * g, :, lanes], table[2 * g + 1, :, lanes]
                fc, fs = table[16 + 2 * i, :, lanes], table[17 + 2 * i, :, lanes]
                green = jnp.concatenate([c * fc, s * fs, s * fc, c * fs], axis=0)
                sums = jnp.dot(coef[i, g], green, preferred_element_type=F32)
                for sg in range(2):
                    total = sums[8 * sg : 8 * sg + 8] * weight[:, lanes]
                    total = total + pltpu.roll(total, 7, 0)
                    total = total + pltpu.roll(total, 6, 0)
                    stage[sg, 2 * g : 2 * g + 1, lanes] = total[4:5]
                    stage[sg, 2 * g + 1 : 2 * g + 2, lanes] = total[0:1]
        for sg in range(2):
            for k in range(4):
                part_out[(step * 2 + sg) * 4 + k] = stage[sg, :, k * 128 : (k + 1) * 128].astype(BF)
        for sg in range(2):
            zt = i if sg == 0 else 7 - i
            for k in range(4):
                xt = (x + k) % 4
                source = part_out.at[(step * 2 + sg) * 4 + xt]
                target = part_in.at[sg, u]

                def send(source=source, target=target, ut=xt * 8 + zt):
                    pltpu.make_async_remote_copy(
                        src_ref=source,
                        dst_ref=target,
                        send_sem=part_sems.at[0],
                        recv_sem=part_sems.at[1],
                        device_id={"vol": ut},
                        device_id_type=MESH,
                    ).start()

                if k:
                    send()
                else:
                    pl.when(zt != z)(send)

                    @pl.when(zt == z)
                    def _(source=source, target=target):
                        pltpu.make_async_copy(source, target, part_sems.at[1]).start()

        return carry

    lax.fori_loop(0, 8, one_fine, 0)

    row = lax.broadcasted_iota(jnp.int32, (128, 32), 0)
    col = lax.broadcasted_iota(jnp.int32, (128, 32), 1)
    bin_of = core * 128 + ((col % 16) // 2 * 2 + 1 - col // 16) * 8 + z
    begin, begins, counts = jnp.int32(0), jnp.zeros_like(row), jnp.zeros_like(row)
    own_begin = jnp.int32(0)
    for m in range(nars):
        amount = counts_ref[m]
        begins = jnp.where(row // 8 == m, begin, begins)
        counts = jnp.where(row // 8 == m, amount, counts)
        own_begin = own_begin + jnp.where(m < n, amount, 0)
        begin = begin + amount
    seat = bin_of - begins
    ahead = seat - (row % 8) // 2 * 8
    chosen = (row % 2 == col % 2) & (ahead >= 0) & (ahead < 8) & (seat < counts)
    chosen = jnp.where(chosen, 1.0, 0.0).astype(BF)

    pltpu.make_async_copy(part_in, part_in, part_sems.at[1]).wait()
    sums = []
    for sg in range(2):

        def add(at, total, sg=sg):
            return total + part_in[sg, at].astype(F32)

        sums.append(lax.fori_loop(1, vols, add, part_in[sg, 0].astype(F32), unroll=True))
    total = jnp.concatenate(sums, axis=0)
    r = lax.broadcasted_iota(jnp.int32, (32, 128), 0)
    b = core * 128 + ((r % 16) // 2 * 2 + 1 - r // 16) * 8 + z
    scale = (b + 1).astype(F32) * (1.0 / math.sqrt(32768.0) / NF)
    total = total * jnp.where(r % 2 == 0, -scale, scale)
    upper = total.astype(BF)
    lower = (total - upper.astype(F32)).astype(BF)
    slots = jnp.dot(chosen, upper, preferred_element_type=F32)
    slots = slots + jnp.dot(chosen, lower, preferred_element_type=F32)
    for m in range(nars):
        slot_out[m] = slots[8 * m : 8 * m + 8]
    own_slot = pltpu.make_async_copy(slot_out.at[n], slot_in.at[n], slot_sems.at[1])
    own_slot.start()

    def send_slot(k, carry):
        m = (n + k) % nars
        pltpu.make_async_remote_copy(
            src_ref=slot_out.at[m],
            dst_ref=slot_in.at[n],
            send_sem=slot_sems.at[0],
            recv_sem=slot_sems.at[1],
            device_id={"nar": m},
            device_id_type=MESH,
        ).start()
        return carry

    lax.fori_loop(1, nars, send_slot, 0)
    pltpu.make_async_copy(slot_in, slot_in, slot_sems.at[1]).wait()
    tile = slot_in[0]
    for m in range(1, nars):
        tile = tile + slot_in[m]

    residue = (z - own_begin + NF) % 8
    for zt in range(8):
        held = jnp.where(residue == zt, 1.0, 0.0) * tile
        for xt in range(4):
            last_out[zt * 4 + xt] = held[2 * xt : 2 * xt + 2]
    own_last = pltpu.make_async_copy(last_out.at[z * 4 + x], last_in.at[z * 4 + x], last_sems.at[1])
    own_last.start()

    def send_last(k, carry):
        ut = (u + k) % vols
        pltpu.make_async_remote_copy(
            src_ref=last_out.at[(ut % 8) * 4 + ut // 8],
            dst_ref=last_in.at[z * 4 + x],
            send_sem=last_sems.at[0],
            recv_sem=last_sems.at[1],
            device_id={"vol": ut},
            device_id_type=MESH,
        ).start()
        return carry

    lax.fori_loop(1, vols, send_last, 0)
    pltpu.make_async_copy(last_in, last_in, last_sems.at[1]).wait()
    for xt in range(4):
        chunk = last_in[xt]
        for zt in range(1, 8):
            chunk = chunk + last_in[zt * 4 + xt]
        out_ref[xt] = chunk

    sent = part_out.at[pl.ds(0, 62)]
    pltpu.make_async_copy(sent, sent, part_sems.at[0]).wait()
    sent = slot_out.at[pl.ds(0, 15)]
    pltpu.make_async_copy(sent, sent, slot_sems.at[0]).wait()
    sent = last_out.at[pl.ds(0, 31)]
    pltpu.make_async_copy(sent, sent, last_sems.at[0]).wait()


def per_device(series, send_rows, bin_counts, observer_cells):
    in_vmem = pl.BlockSpec(memory_space=pltpu.VMEM)
    chunks = pl.pallas_call(
        kernel,
        out_shape=jax.ShapeDtypeStruct((4, 2, 128), F32),
        in_specs=[pl.BlockSpec(memory_space=pltpu.SMEM)] + [in_vmem] * 4,
        out_specs=in_vmem,
        scratch_shapes=[
            pltpu.VMEM((2048, 128), F32),
            pltpu.VMEM((1024, 128), F32),
            pltpu.VMEM((1024, 128), BF),
            pltpu.VMEM((1024, 128), BF),
            pltpu.VMEM((3, 128, 128), F32),
            pltpu.VMEM((3, 8, OBS), F32),
            pltpu.VMEM((8, OBS), F32),
            pltpu.VMEM((32, 128, OBS), BF),
            pltpu.VMEM((8, 8, 16, 512), BF),
            pltpu.VMEM((2, 16, OBS), F32),
            pltpu.VMEM((64, 16, 128), BF),
            pltpu.VMEM((2, 32, 16, 128), BF),
            pltpu.VMEM((16, 8, 128), F32),
            pltpu.VMEM((16, 8, 128), F32),
            pltpu.VMEM((32, 2, 128), F32),
            pltpu.VMEM((32, 2, 128), F32),
            pltpu.SemaphoreType.DMA((2,)),
            pltpu.SemaphoreType.DMA((2,)),
            pltpu.SemaphoreType.DMA((2,)),
            pltpu.SemaphoreType.DMA((2,)),
        ],
        compiler_params=pltpu.CompilerParams(
            collective_id=0, has_side_effects=True, vmem_limit_bytes=48 << 20
        ),
    )(
        bin_counts,
        series,
        send_rows.reshape(1, -1),
        observer_cells,
        jnp.asarray(dft_rows()),
    )
    return chunks.transpose(1, 0, 2).reshape(1, 1, 2, OBS)


def solution(mesh):
    placed = (P(("vol", "nar"), None), P("vol", "nar", None), P(), P())
    return jax.shard_map(
        per_device,
        mesh=mesh,
        in_specs=placed,
        out_specs=P("nar", "vol", None, None),
        check_vma=False,
    )
```

profile of v0, /device:TPU:1, one launch (start us, length us, event | category | flops | bytes accessed | tf_op | source)
XLA Modules:
  0.0 46.5 jit_solution(11429393122174348350)
XLA Ops:
  0.0 0.0 copy-start.3
  0.0 0.0 copy-start.4
  0.0 0.7 %copy-done.3 = s32[16]{0:T(128)S(1)} copy-done((s32[16]{0:T(128)S(1)}, s32[16]{0:T(128)}, u32[]{:S(2)}) %copy-start.3) | copy-done | bytes 88
  0.7 0.0 copy-done.4
  0.7 0.0 copy-start
  0.7 1.0 %copy-done = bf16[512,512]{1,0:T(8,128)(2,1)S(1)} copy-done((bf16[512,512]{1,0:T(8,128)(2,1)S(1)}, bf16[512,512]{1,0:T(8,128)(2,1)}, u32[]{:S(2)}) %copy-start) | copy-done | bytes 524312
  1.7 0.0 copy-start.1
  1.7 0.9 %copy-done.1 = bf16[64,2048]{1,0:T(8,128)(2,1)S(1)} copy-done((bf16[64,2048]{1,0:T(8,128)(2,1)S(1)}, bf16[64,2048]{1,0:T(8,128)(2,1)}, u32[]{:S(2)}) %copy-start.1) | copy-done | bytes 262168
  2.7 0.0 copy-start.2
  2.7 0.7 %copy-done.2 = s32[2,512]{1,0:T(2,128)S(1)} copy-done((s32[2,512]{1,0:T(2,128)S(1)}, s32[2,512]{1,0:T(2,128)}, u32[]{:S(2)}) %copy-start.2) | copy-done | bytes 4120
  3.4 42.6 %shard_map.55 = f32[4,2,128]{2,1,0:T(2,128)S(1)} custom-call(s32[16]{0:T(128)S(1)} %copy-done.3, bf16[64,2048]{1,0:T(8,128)(2,1)S(1)} %copy-done.1, s32[1,64]{1,0:T(1,128)S(1)} %bitcast.5, s32[2,512]{1,0:T(2,128)S(1)} %copy-done.2, bf16[512,512]{1,0:T(8,128)(2,1)S(1)} %copy-done), custom_call_target="tpu_custom_call" | custom-call | tf_op jit(solution)/shard_map/pallas_call | solution.py:354
  45.9 0.6 %copy.7 = f32[1,1,2,512]{3,2,1,0:T(2,128)} copy(f32[1,1,2,512]{3,2,1,0:T(2,128)S(1)} %bitcast.4) | data formatting | bytes 8192
Async XLA Ops:
  0.0 0.7 %copy-start.3 = (s32[16]{0:T(128)S(1)}, s32[16]{0:T(128)}, u32[]{:S(2)}) copy-start(s32[16]{0:T(128)} %counts_ref.1) | copy-start | bytes 196
  0.0 0.7 %copy-start.4 = (s32[1,1,64]{2,1,0:T(1,128)S(1)}, s32[1,1,64]{2,1,0:T(1,128)}, u32[]{:S(2)}) copy-start(s32[1,1,64]{2,1,0:T(1,128)} %param.6) | copy-start | bytes 772
  0.7 1.0 %copy-start = (bf16[512,512]{1,0:T(8,128)(2,1)S(1)}, bf16[512,512]{1,0:T(8,128)(2,1)}, u32[]{:S(2)}) copy-start(bf16[512,512]{1,0:T(8,128)(2,1)} %constant.2.clone.dft_ref) | copy-start | bytes 1572868
  1.7 0.9 %copy-start.1 = (bf16[64,2048]{1,0:T(8,128)(2,1)S(1)}, bf16[64,2048]{1,0:T(8,128)(2,1)}, u32[]{:S(2)}) copy-start(bf16[64,2048]{1,0:T(8,128)(2,1)} %series_ref.1) | copy-start | bytes 786436
  2.7 0.7 %copy-start.2 = (s32[2,512]{1,0:T(2,128)S(1)}, s32[2,512]{1,0:T(2,128)}, u32[]{:S(2)}) copy-start(s32[2,512]{1,0:T(2,128)} %cells_ref.1) | copy-start | bytes 12292
where the time goes:
time: 46.8 us; the launch traced here: 46.5 us
  Pallas kernels  42.6 us (91%)
  local copies, waits for them, and re-layouts  3.94 us (8%)
    pallas_call x1, Pallas kernels, per_device(): pl.pallas_call(kernel, out_shape=jax.ShapeDtypeStruct((4, 2, 128), F32),...  42.6 us
    unnamed x11, local copies, waits for them, and re-layouts  3.94 us

commit v1 on v0

v1 whole, which is shorter than its diff:
```python
import math

import jax
import jax.numpy as jnp
import ml_dtypes
import numpy as np
from jax import lax
from jax.experimental import pallas as pl
from jax.experimental.pallas import tpu as pltpu
from jax.sharding import PartitionSpec as P

NT = 512
NF = 256
NQ = 4
OBS = 512
WAVE_STEP = 0.05
BF = jnp.bfloat16
F32 = jnp.float32
MESH = pl.DeviceIdType.MESH


def dft_rows():
    steps = np.arange(NT, dtype=np.int64)
    turns = (np.arange(1, NF + 1, dtype=np.int64)[:, None] * steps[None, :]) % NT
    angle = turns.astype(np.float32) * np.float32(2.0 * math.pi / NT)
    table = np.stack([np.cos(angle), -np.sin(angle)], axis=1)
    return table.reshape(2 * NF, NT).astype(ml_dtypes.bfloat16)


SIN_TERMS = [(-1.0) ** i / math.factorial(2 * i + 1) for i in range(7)]
COS_TERMS = [(-1.0) ** i / math.factorial(2 * i) for i in range(8)]


def polynomial(terms, square):
    total = terms[-1]
    for term in terms[-2::-1]:
        total = total * square + term
    return total


def cos_sin(turns):
    half = (turns - jnp.round(turns)) * math.pi
    square = half * half
    s = half * polynomial(SIN_TERMS, square)
    c = polynomial(COS_TERMS, square)
    return 1.0 - 2.0 * s * s, 2.0 * s * c


def times(one, other):
    return one[0] * other[0] - one[1] * other[1], one[0] * other[1] + one[1] * other[0]


def squared(one):
    return 1.0 - 2.0 * one[1] * one[1], 2.0 * one[0] * one[1]


def modulo(value, base):
    rest = value - (value.astype(F32) * (1.0 / base)).astype(jnp.int32) * base
    rest = jnp.where(rest < 0, rest + base, rest)
    return jnp.where(rest >= base, rest - base, rest)


def kernel(
    counts_hbm,
    series_hbm,
    listing_hbm,
    cells_hbm,
    dft_hbm,
    out_ref,
    counts_ref,
    series_ref,
    listing_ref,
    cells_ref,
    dft_ref,
    spec,
    own,
    swap_out,
    swap_in,
    place,
    facing,
    weight,
    table,
    coef,
    stage,
    part_out,
    part_in,
    slot_out,
    slot_in,
    last_out,
    last_in,
    swap_sems,
    sent_sem,
    part_sems,
    slot_sems,
    last_sems,
    load_sems,
):
    u = lax.axis_index("vol")
    n = lax.axis_index("nar")
    x, z = u // 8, u % 8
    core = n % 2
    vols, nars = 32, 16

    loads = [
        pltpu.make_async_copy(source, target, load_sems.at[i])
        for i, (source, target) in enumerate(
            (
                (dft_hbm, dft_ref),
                (series_hbm, series_ref),
                (listing_hbm, listing_ref),
                (cells_hbm, cells_ref),
                (counts_hbm, counts_ref),
            )
        )
    ]
    for load in loads:
        load.start()

    barrier = pltpu.get_barrier_semaphore()

    def greet_vol(k, carry):
        pl.semaphore_signal(barrier, inc=1, device_id={"vol": (u + k) % vols}, device_id_type=MESH)
        return carry

    def greet_nar(k, carry):
        pl.semaphore_signal(barrier, inc=1, device_id={"nar": (n + k) % nars}, device_id_type=MESH)
        return carry

    lax.fori_loop(1, vols, greet_vol, 0)
    lax.fori_loop(1, nars, greet_nar, 0)
    for load in loads:
        load.wait()

    pick = lax.broadcasted_iota(jnp.int32, (64, 64), 0) == listing_ref[...]
    surface = lax.dot_general(
        jnp.where(pick, 1.0, 0.0).astype(BF),
        series_ref[...],
        (((0,), (0,)), ((), ())),
        preferred_element_type=F32,
    ).astype(BF)
    rows = jnp.concatenate([surface[:, q * NT : (q + 1) * NT] for q in range(NQ)], axis=0)

    def transform(half):
        lines = dft_ref[pl.ds(pl.multiple_of(half * 256, 256), 256), :]
        spectra = lax.dot_general(lines, rows, (((1,), (1,)), ((), ())), preferred_element_type=F32)
        spectra = spectra * (1.0 / math.sqrt(NT))
        for q in range(NQ):
            both = spectra[:, q // 2 * 128 : q // 2 * 128 + 128]
            spec[pl.ds(q, 256, stride=NQ), :] = jnp.where(core == q % 2, both, pltpu.roll(both, 64, 1))

    transform(1 - core)
    swap_out[...] = spec[...].astype(BF)
    pl.semaphore_wait(barrier, vols + nars - 2)
    swap = pltpu.make_async_remote_copy(
        src_ref=swap_out,
        dst_ref=swap_in,
        send_sem=swap_sems.at[0],
        recv_sem=swap_sems.at[1],
        device_id={"nar": n + 1 - 2 * core},
        device_id_type=MESH,
    )
    swap.start()
    transform(core)

    slab = u * 8 + n // 2
    point = slab * 128 + lax.broadcasted_iota(jnp.int32, (128, 128), 0)
    c, s = cos_sin(modulo(point * 1597, 8191).astype(F32) * (1.0 / 8191.0))
    place[0] = 20.0 * c
    place[1] = 20.0 * s
    place[2] = slab.astype(F32) * 0.5 + modulo(point * 613, 127).astype(F32) * (0.37 / 127.0)
    cells = cells_ref[...].astype(F32)
    polar = cos_sin((cells[0:1] + 0.5) * (1.0 / 256.0))
    azimuth = cos_sin(cells[1:2] * (1.0 / 128.0))
    facing[0] = jnp.broadcast_to(polar[1] * azimuth[0], (8, OBS))
    facing[1] = jnp.broadcast_to(polar[1] * azimuth[1], (8, OBS))
    facing[2] = jnp.broadcast_to(polar[0], (8, OBS))
    term = lax.broadcasted_iota(jnp.int32, (8, OBS), 0) % NQ
    weight[...] = jnp.where(
        term == 0,
        1.0,
        jnp.where(term == 1, facing[0], jnp.where(term == 2, facing[1], facing[2])),
    )

    def fill(at, carry):
        rows16 = pl.ds(pl.multiple_of((at // 2) * 16, 16), 16)
        lanes = pl.ds(pl.multiple_of((at % 2) * 256, 256), 256)
        dotted = 0.0
        for axis in range(3):
            spot = place[axis, rows16, :]
            look = facing[axis, :, lanes]
            dotted = dotted + jnp.concatenate([spot, spot], axis=1) * jnp.concatenate([look, look], axis=0)
        turns = dotted * (WAVE_STEP / (2.0 * math.pi))

        def keep(index, value):
            table[index, rows16, lanes] = value[0].astype(BF)
            table[index + 1, rows16, lanes] = value[1].astype(BF)

        step = cos_sin(turns)
        coarse = cos_sin(turns * (core.astype(F32) * 128.0 + 61.0))
        keep(0, coarse)
        for r in range(1, 8):
            coarse = times(coarse, step)
            keep(2 * r, coarse)
        fine = squared(squared(step))
        step = squared(fine)
        keep(16, fine)
        for j in range(1, 8):
            fine = times(fine, step)
            keep(16 + 2 * j, fine)
        return carry

    lax.fori_loop(0, 16, fill, 0)

    swap.wait()
    held_here = lax.broadcasted_iota(jnp.int32, (64, 128), 1) // 64 == core

    def join(at, carry):
        here = pl.ds(pl.multiple_of(at * 64, 64), 64)
        own[here, :] = jnp.where(held_here, spec[here, :], swap_in[here, :].astype(F32))
        return carry

    lax.fori_loop(0, 16, join, 0)
    sign = jnp.where(lax.broadcasted_iota(jnp.int32, (8, 128), 0) < 4, 1.0, -1.0)

    def lay(r, carry):
        for j in range(8):
            high = own[pl.ds(pl.multiple_of((r + 8 * (8 + j)) * 8, 8), 8), :]
            low = own[pl.ds(pl.multiple_of((r + 8 * (7 - j)) * 8, 8), 8), :]
            high2 = pltpu.roll(high, 4, 0) * sign
            low2 = pltpu.roll(low, 4, 0) * sign
            blocks = ((high, low), (-high, low), (high2, low2), (high2, -low2))
            for k, both in enumerate(blocks):
                coef[r, j, :, pl.ds(k * 128, 128)] = jnp.concatenate(both, axis=0).astype(BF)
        return carry

    lax.fori_loop(0, 8, lay, 0)

    def one_plane(step, carry):
        zt = (z + 4 + (1 - 2 * (step % 2)) * ((step + 1) // 2)) % 8
        for part in range(2):
            half = (x // 2 + 1 + part) % 2
            lanes = pl.ds(pl.multiple_of(half * 256, 256), 256)
            for j in range(8):
                c, s = table[2 * zt, :, lanes], table[2 * zt + 1, :, lanes]
                fc, fs = table[16 + 2 * j, :, lanes], table[17 + 2 * j, :, lanes]
                green = jnp.concatenate([c * fc, s * fs, s * fc, c * fs], axis=0)
                sums = jnp.dot(coef[zt, j], green, preferred_element_type=F32)
                for sg, k in enumerate((8 + j, 7 - j)):
                    total = sums[8 * sg : 8 * sg + 8] * weight[:, lanes]
                    total = total + pltpu.roll(total, 7, 0)
                    total = total + pltpu.roll(total, 6, 0)
                    stage[part, 2 * k : 2 * k + 1, :] = total[4:5]
                    stage[part, 2 * k + 1 : 2 * k + 2, :] = total[0:1]
            for k in range(2):
                xt = 2 * half + (x + 1 + k) % 2
                chosen = jnp.where((x + 1 + k) % 2 == 0, stage[part, :, 0:128], stage[part, :, 128:256])
                part_out[step * 4 + xt] = chosen.astype(BF)

                def send(xt=xt):
                    pltpu.make_async_remote_copy(
                        src_ref=part_out.at[step * 4 + xt],
                        dst_ref=part_in.at[step * 4 + x],
                        send_sem=sent_sem.at[0],
                        recv_sem=part_sems.at[step],
                        device_id={"vol": xt * 8 + zt},
                        device_id_type=MESH,
                    ).start()

                if part == 1 and k == 1:
                    pl.when(step < 7)(send)
                else:
                    send()
        return carry

    lax.fori_loop(0, 8, one_plane, 0)
    part_in[28 + x] = part_out[28 + x]

    row = lax.broadcasted_iota(jnp.int32, (128, 32), 0)
    col = lax.broadcasted_iota(jnp.int32, (128, 32), 1)
    bin_of = core * 128 + col // 2 * 8 + z
    begin, begins, counts = jnp.int32(0), jnp.zeros_like(row), jnp.zeros_like(row)
    own_begin = jnp.int32(0)
    for m in range(nars):
        amount = counts_ref[m]
        begins = jnp.where(row // 8 == m, begin, begins)
        counts = jnp.where(row // 8 == m, amount, counts)
        own_begin = own_begin + jnp.where(m < n, amount, 0)
        begin = begin + amount
    seat = bin_of - begins
    ahead = seat - (row % 8) // 2 * 8
    chosen = (row % 2 == col % 2) & (ahead >= 0) & (ahead < 8) & (seat < counts)
    chosen = jnp.where(chosen, 1.0, 0.0).astype(BF)

    total = jnp.zeros((32, 128), F32)
    for step in range(8):
        arrived = part_in.at[pl.ds(step * 4, 4 if step < 7 else 3)]
        pltpu.make_async_copy(arrived, arrived, part_sems.at[step]).wait()
        for xs in range(4):
            total = total + part_in[step * 4 + xs].astype(F32)
    r = lax.broadcasted_iota(jnp.int32, (32, 128), 0)
    b = core * 128 + r // 2 * 8 + z
    scale = (b + 1).astype(F32) * (1.0 / math.sqrt(32768.0) / NF)
    total = total * jnp.where(r % 2 == 0, -scale, scale)
    upper = total.astype(BF)
    lower = (total - upper.astype(F32)).astype(BF)
    slots = jnp.dot(chosen, upper, preferred_element_type=F32)
    slots = slots + jnp.dot(chosen, lower, preferred_element_type=F32)
    for m in range(nars):
        slot_out[m] = slots[8 * m : 8 * m + 8]
    own_slot = pltpu.make_async_copy(slot_out.at[n], slot_in.at[n], slot_sems.at[1])
    own_slot.start()

    def send_slot(at, carry):
        m = (n + 8 + (1 - 2 * (at % 2)) * ((at + 1) // 2)) % nars
        pltpu.make_async_remote_copy(
            src_ref=slot_out.at[m],
            dst_ref=slot_in.at[n],
            send_sem=slot_sems.at[0],
            recv_sem=slot_sems.at[1],
            device_id={"nar": m},
            device_id_type=MESH,
        ).start()
        return carry

    lax.fori_loop(0, nars - 1, send_slot, 0)
    pltpu.make_async_copy(slot_in, slot_in, slot_sems.at[1]).wait()
    tile = slot_in[0]
    for m in range(1, nars):
        tile = tile + slot_in[m]

    residue = (z - own_begin + NF) % 8
    for zt in range(8):
        held = jnp.where(residue == zt, 1.0, 0.0) * tile
        for xt in range(4):
            last_out[zt * 4 + xt] = held[2 * xt : 2 * xt + 2]
    own_last = pltpu.make_async_copy(last_out.at[z * 4 + x], last_in.at[z * 4 + x], last_sems.at[1])
    own_last.start()

    away = [(kx, kz) for kx in range(4) for kz in range(8) if kx or kz]
    for kx, kz in sorted(away, key=lambda k: -min(k[0], 4 - k[0]) - min(k[1], 8 - k[1])):
        xt, zt = (x + kx) % 4, (z + kz) % 8
        pltpu.make_async_remote_copy(
            src_ref=last_out.at[zt * 4 + xt],
            dst_ref=last_in.at[z * 4 + x],
            send_sem=last_sems.at[0],
            recv_sem=last_sems.at[1],
            device_id={"vol": xt * 8 + zt},
            device_id_type=MESH,
        ).start()
    pltpu.make_async_copy(last_in, last_in, last_sems.at[1]).wait()
    for xt in range(4):
        chunk = last_in[xt]
        for zt in range(1, 8):
            chunk = chunk + last_in[zt * 4 + xt]
        out_ref[xt] = chunk

    sent = part_out.at[pl.ds(0, 31)]
    pltpu.make_async_copy(sent, sent, sent_sem.at[0]).wait()
    sent = slot_out.at[pl.ds(0, 15)]
    pltpu.make_async_copy(sent, sent, slot_sems.at[0]).wait()
    sent = last_out.at[pl.ds(0, 31)]
    pltpu.make_async_copy(sent, sent, last_sems.at[0]).wait()


def per_device(series, send_rows, bin_counts, observer_cells):
    in_vmem = pl.BlockSpec(memory_space=pltpu.VMEM)
    chunks = pl.pallas_call(
        kernel,
        out_shape=jax.ShapeDtypeStruct((4, 2, 128), F32),
        in_specs=[pl.BlockSpec(memory_space=pl.ANY)] * 5,
        out_specs=in_vmem,
        scratch_shapes=[
            pltpu.SMEM((16,), jnp.int32),
            pltpu.VMEM((64, NQ * NT), BF),
            pltpu.VMEM((1, 64), jnp.int32),
            pltpu.VMEM((2, OBS), jnp.int32),
            pltpu.VMEM((2 * NF, NT), BF),
            pltpu.VMEM((1024, 128), F32),
            pltpu.VMEM((1024, 128), F32),
            pltpu.VMEM((1024, 128), BF),
            pltpu.VMEM((1024, 128), BF),
            pltpu.VMEM((3, 128, 128), F32),
            pltpu.VMEM((3, 8, OBS), F32),
            pltpu.VMEM((8, OBS), F32),
            pltpu.VMEM((32, 128, OBS), BF),
            pltpu.VMEM((8, 8, 16, 512), BF),
            pltpu.VMEM((2, 32, 256), F32),
            pltpu.VMEM((32, 32, 128), BF),
            pltpu.VMEM((32, 32, 128), BF),
            pltpu.VMEM((16, 8, 128), F32),
            pltpu.VMEM((16, 8, 128), F32),
            pltpu.VMEM((32, 2, 128), F32),
            pltpu.VMEM((32, 2, 128), F32),
            pltpu.SemaphoreType.DMA((2,)),
            pltpu.SemaphoreType.DMA((1,)),
            pltpu.SemaphoreType.DMA((8,)),
            pltpu.SemaphoreType.DMA((2,)),
            pltpu.SemaphoreType.DMA((2,)),
            pltpu.SemaphoreType.DMA((5,)),
        ],
        compiler_params=pltpu.CompilerParams(
            collective_id=0, has_side_effects=True, vmem_limit_bytes=56 << 20
        ),
    )(
        bin_counts,
        series,
        send_rows.reshape(1, -1),
        observer_cells,
        jnp.asarray(dft_rows()),
    )
    return chunks.transpose(1, 0, 2).reshape(1, 1, 2, OBS)


def solution(mesh):
    placed = (P(("vol", "nar"), None), P("vol", "nar", None), P(), P())
    return jax.shard_map(
        per_device,
        mesh=mesh,
        in_specs=placed,
        out_specs=P("nar", "vol", None, None),
        check_vma=False,
    )
```

time: 46.8 us -> 41.3 us (0.88)
  Pallas kernels: 42.6 us -> 39.9 us
  local copies, waits for them, and re-layouts: 3.94 us -> 1.28 us
    pallas_call x1, Pallas kernels: 42.6 us -> 39.9 us  [per_device(): pl.pallas_call(kernel, out_shape=jax.ShapeDtypeStruct((4, 2, 128), F32),...]
    unnamed x11 -> x1, local copies, waits for them, and re-layouts: 3.94 us -> 1.28 us
where the time goes in v1:
time: 41.3 us; the launch traced here: 41.2 us
  Pallas kernels  39.9 us (97%)
  local copies, waits for them, and re-layouts  1.28 us (3%)
    pallas_call x1, Pallas kernels, per_device(): pl.pallas_call(kernel, out_shape=jax.ShapeDtypeStruct((4, 2, 128), F32),...  39.9 us
    unnamed x1, local copies, waits for them, and re-layouts  1.28 us

profile of v1, /device:TPU:1, one launch (start us, length us, event | category | flops | bytes accessed | tf_op | source)
XLA Modules:
  0.0 41.2 jit_solution(12863749384909083189)
XLA Ops:
  0.0 39.9 %shard_map.55 = f32[4,2,128]{2,1,0:T(2,128)} custom-call(s32[16]{0:T(128)} %counts_hbm.1, bf16[64,2048]{1,0:T(8,128)(2,1)} %series_hbm.1, s32[1,64]{1,0:T(1,128)} %bitcast.5, s32[2,512]{1,0:T(2,128)} %cells_hbm.1, bf16[512,512]{1,0:T(8,128)(2,1)} %constant.2.clone.dft_hbm), custom_call_target="tpu_custom_call" | custom-call | tf_op jit(solution)/shard_map/pallas_call | solution.py:367
  39.9 1.3 %copy.7 = f32[1,1,2,512]{3,2,1,0:T(2,128)} copy(f32[1,1,2,512]{3,2,1,0:T(2,128)} %bitcast.4) | data formatting | bytes 8192

commit v2 on v1

v2 whole, which is shorter than its diff:
```python
import math

import jax
import jax.numpy as jnp
import ml_dtypes
import numpy as np
from jax import lax
from jax.experimental import pallas as pl
from jax.experimental.pallas import tpu as pltpu
from jax.sharding import PartitionSpec as P

NT = 512
NF = 256
NQ = 4
OBS = 512
WAVE_STEP = 0.05
BF = jnp.bfloat16
F32 = jnp.float32
MESH = pl.DeviceIdType.MESH


def dft_rows():
    steps = np.arange(NT, dtype=np.int64)
    turns = (np.arange(1, NF + 1, dtype=np.int64)[:, None] * steps[None, :]) % NT
    angle = turns.astype(np.float32) * np.float32(2.0 * math.pi / NT)
    table = np.stack([np.cos(angle), -np.sin(angle)], axis=1)
    return table.reshape(2 * NF, NT).astype(ml_dtypes.bfloat16)


SIN_TERMS = [(-1.0) ** i / math.factorial(2 * i + 1) for i in range(6)]
COS_TERMS = [(-1.0) ** i / math.factorial(2 * i) for i in range(7)]


def polynomial(terms, square):
    total = terms[-1]
    for term in terms[-2::-1]:
        total = total * square + term
    return total


def cos_sin(turns):
    half = (turns - jnp.round(turns)) * math.pi
    square = half * half
    s = half * polynomial(SIN_TERMS, square)
    c = polynomial(COS_TERMS, square)
    return 1.0 - 2.0 * s * s, 2.0 * s * c


def times(one, other):
    return one[0] * other[0] - one[1] * other[1], one[0] * other[1] + one[1] * other[0]


def squared(one):
    return 1.0 - 2.0 * one[1] * one[1], 2.0 * one[0] * one[1]


def modulo(value, base):
    rest = value - (value.astype(F32) * (1.0 / base)).astype(jnp.int32) * base
    rest = jnp.where(rest < 0, rest + base, rest)
    return jnp.where(rest >= base, rest - base, rest)


def kernel(
    counts_hbm,
    series_hbm,
    listing_hbm,
    cells_hbm,
    dft_hbm,
    out_ref,
    counts_ref,
    series_ref,
    listing_ref,
    cells_ref,
    dft_ref,
    spec,
    swap_out,
    swap_in,
    place,
    facing,
    weight,
    table,
    coef,
    begun,
    picks,
    scale,
    stage,
    part_out,
    part_in,
    relay_out,
    relay_in,
    slot_out,
    slot_in,
    tile,
    last_out,
    last_in,
    swap_sems,
    sent_sem,
    part_sems,
    relay_sems,
    slot_sems,
    last_sems,
    load_sems,
):
    u = lax.axis_index("vol")
    n = lax.axis_index("nar")
    x, z = u // 8, u % 8
    core = n % 2
    y = n // 2
    nars = 16

    loads = [
        pltpu.make_async_copy(source, target, load_sems.at[i])
        for i, (source, target) in enumerate(
            (
                (cells_hbm, cells_ref),
                (counts_hbm, counts_ref),
                (listing_hbm, listing_ref),
                (series_hbm, series_ref),
                (dft_hbm, dft_ref),
            )
        )
    ]
    for load in loads:
        load.start()

    barrier = pltpu.get_barrier_semaphore()

    by_xz = [(a, b) for a in range(4) for b in range(8) if a or b]
    by_xz.sort(key=lambda k: -min(k[0], 4 - k[0]) - min(k[1], 8 - k[1]))
    by_zc = [(a, b) for a in range(8) for b in range(2) if a or b]
    by_zc.sort(key=lambda k: -min(k[0], 8 - k[0]) - k[1])

    def at_xz(a, b):
        return {"vol": (x + a) % 4 * 8 + (z + b) % 8}

    def at_xy(a, b):
        return {"vol": (x + a) % 4 * 8 + z, "nar": (y + b) % 8 * 2 + core}

    def at_zc(a, b):
        return {"vol": x * 8 + (z + a) % 8, "nar": y * 2 + (core + b) % 2}

    met = [(*k, 0, 0) for k in by_xz]
    met += [(k[0], 0, k[1], 0) for k in by_xz if k[1]]
    met += [(0, k[0], 0, k[1]) for k in by_zc if k[1]]
    met.sort(key=lambda k: -min(k[0], 4 - k[0]) - min(k[1], 8 - k[1]) - min(k[2], 8 - k[2]))
    for a, b, c, d in met:
        other = {
            "vol": (x + a) % 4 * 8 + (z + b) % 8,
            "nar": (y + c) % 8 * 2 + (core + d) % 2,
        }
        pl.semaphore_signal(barrier, inc=1, device_id=other, device_id_type=MESH)

    loads[0].wait()
    slab = u * 8 + n // 2
    point = slab * 128 + (lax.broadcasted_iota(jnp.int32, (128, 128), 0) + 64 * core) % 128
    c, s = cos_sin(modulo(point * 1597, 8191).astype(F32) * (1.0 / 8191.0))
    place[0] = 20.0 * c
    place[1] = 20.0 * s
    place[2] = slab.astype(F32) * 0.5 + modulo(point * 613, 127).astype(F32) * (0.37 / 127.0)
    cells = cells_ref[...].astype(F32)
    polar = cos_sin((cells[0:1] + 0.5) * (1.0 / 256.0))
    azimuth = cos_sin(cells[1:2] * (1.0 / 128.0))
    facing[0] = jnp.broadcast_to(polar[1] * azimuth[0], (8, OBS))
    facing[1] = jnp.broadcast_to(polar[1] * azimuth[1], (8, OBS))
    facing[2] = jnp.broadcast_to(polar[0], (8, OBS))
    term = lax.broadcasted_iota(jnp.int32, (8, OBS), 0) % NQ
    weight[...] = jnp.where(
        term == 0,
        1.0,
        jnp.where(term == 1, facing[0], jnp.where(term == 2, facing[1], facing[2])),
    )

    def fill(at, carry):
        rows16 = pl.ds(pl.multiple_of((at // 2) * 16, 16), 16)
        lanes = pl.ds(pl.multiple_of((at % 2) * 256, 256), 256)
        dotted = 0.0
        for axis in range(3):
            spot = place[axis, rows16, :]
            look = facing[axis, :, lanes]
            dotted = dotted + jnp.concatenate([spot, spot], axis=1) * jnp.concatenate([look, look], axis=0)
        turns = dotted * (WAVE_STEP / (2.0 * math.pi))

        def keep(index, value):
            table[index, rows16, lanes] = value[0].astype(BF)
            table[index + 1, rows16, lanes] = value[1].astype(BF)

        def onward(index, before, now, step):
            twice = 2.0 * step[0]
            keep(index, now)
            for k in range(1, 8):
                after = twice * now[0] - before[0], twice * now[1] - before[1]
                before, now = now, after
                keep(index + 2 * k, now)

        step = cos_sin(turns)
        coarse = cos_sin(turns * (core.astype(F32) * 128.0 + 61.0))
        onward(0, times(coarse, (step[0], -step[1])), coarse, step)
        fine = squared(squared(step))
        onward(16, (fine[0], -fine[1]), fine, squared(fine))
        return carry

    lax.fori_loop(0, 16, fill, 0)

    loads[1].wait()
    row = lax.broadcasted_iota(jnp.int32, (128, 32), 0)
    col = lax.broadcasted_iota(jnp.int32, (128, 32), 1)
    bin_of = core * 128 + col // 2 * 8 + z
    owner = row // 16 * 2 + row % 4 // 2
    begin, begins, counts = jnp.int32(0), jnp.zeros_like(row), jnp.zeros_like(row)
    own_begins = [jnp.int32(0), jnp.int32(0)]
    for m in range(nars):
        amount = counts_ref[m]
        begins = jnp.where(owner == m, begin, begins)
        counts = jnp.where(owner == m, amount, counts)
        for k in range(2):
            own_begins[k] = own_begins[k] + jnp.where(m < 2 * y + k, amount, 0)
        begin = begin + amount
    seat = bin_of - begins
    ahead = seat - row // 4 % 4 * 8
    chosen = (row % 2 == col % 2) & (ahead >= 0) & (ahead < 8) & (seat < counts)
    picks[...] = jnp.where(chosen, 1.0, 0.0).astype(BF)
    r = lax.broadcasted_iota(jnp.int32, (32, 128), 0)
    b = core * 128 + r // 2 * 8 + z
    amount = (b + 1).astype(F32) * (1.0 / math.sqrt(32768.0) / NF)
    scale[...] = jnp.where(r % 2 == 0, -amount, amount)

    for load in loads[2:]:
        load.wait()
    pick = lax.broadcasted_iota(jnp.int32, (64, 64), 0) == listing_ref[...]
    surface = lax.dot_general(
        jnp.where(pick, 1.0, 0.0).astype(BF),
        series_ref[...],
        (((0,), (0,)), ((), ())),
        preferred_element_type=F32,
    ).astype(BF)
    rows = jnp.concatenate([surface[:, q * NT : (q + 1) * NT] for q in range(NQ)], axis=0)

    def transform(half):
        lines = dft_ref[pl.ds(pl.multiple_of(half * 256, 256), 256), :]
        spectra = lax.dot_general(lines, rows, (((1,), (1,)), ((), ())), preferred_element_type=F32)
        spectra = spectra * (1.0 / math.sqrt(NT))
        first = lax.broadcasted_iota(jnp.int32, (256, 128), 1) < 64
        for q in range(NQ):
            both = spectra[:, q // 2 * 128 : q // 2 * 128 + 128]
            flipped = pltpu.roll(both, 64, 1)
            twice = jnp.where(first, flipped, both) if q % 2 else jnp.where(first, both, flipped)
            spec[pl.ds(q, 256, stride=NQ), :] = twice

    transform(1 - core)
    swap_out[...] = spec[...].astype(BF)
    transform(core)

    sign = jnp.where(lax.broadcasted_iota(jnp.int32, (8, 128), 0) < 4, 1.0, -1.0)
    turn = jnp.where(lax.broadcasted_iota(jnp.int32, (8, 128), 1) < 64, 1.0, -1.0)

    def lay_at(lane):
        def lay(r, carry):
            for j in range(8):
                high = spec[pl.ds(pl.multiple_of((r + 8 * (8 + j)) * 8, 8), 8), :]
                low = spec[pl.ds(pl.multiple_of((r + 8 * (7 - j)) * 8, 8), 8), :]
                high2 = pltpu.roll(high, 4, 0) * sign
                low2 = pltpu.roll(low, 4, 0) * sign
                blocks = ((high * turn, low), (high2, low2 * turn))
                for k, both in enumerate(blocks):
                    lanes = pl.ds(lane + k * 128, 128)
                    coef[r, j, :, lanes] = jnp.concatenate(both, axis=0).astype(BF)
            return carry

        lax.fori_loop(0, 8, lay, 0)

    def plane_of(step):
        return (z + 4 + (1 - 2 * (step % 2)) * ((step + 1) // 2)) % 8

    def products(zt, j, lanes, first, last):
        green = []
        for block in range(first, last):
            points = pl.ds(block * 64, 64)
            c, s = table[2 * zt, points, lanes], table[2 * zt + 1, points, lanes]
            fc, fs = table[16 + 2 * j, points, lanes], table[17 + 2 * j, points, lanes]
            green += [c * fc, s * fs, s * fc, c * fs]
        left = coef[zt, j, :, pl.ds(first * 256, (last - first) * 256)]
        return jnp.dot(left, jnp.concatenate(green, axis=0), preferred_element_type=F32)

    def begin_plane(step, carry):
        zt = plane_of(step)
        for half in range(2):
            lanes = pl.ds(half * 256, 256)
            for j in range(8):
                begun[step, j, :, lanes] = products(zt, j, lanes, 0, 1)
        return carry

    def finish_plane(step, carry, first, relayed=False):
        zt = plane_of(step)
        for part in range(2):
            half = (x // 2 + 1 + part) % 2
            lanes = pl.ds(pl.multiple_of(half * 256, 256), 256)
            for j in range(8):
                sums = products(zt, j, lanes, first, 2)
                if first:
                    sums = sums + begun[step, j, :, lanes]
                for sg, k in enumerate((8 + j, 7 - j)):
                    total = sums[8 * sg : 8 * sg + 8] * weight[:, lanes]
                    total = total + pltpu.roll(total, 7, 0)
                    total = total + pltpu.roll(total, 6, 0)
                    stage[part, 2 * k : 2 * k + 1, :] = total[4:5]
                    stage[part, 2 * k + 1 : 2 * k + 2, :] = total[0:1]
            for k in range(2):
                xt = 2 * half + (x + 1 + k) % 2
                chosen = jnp.where((x + 1 + k) % 2 == 0, stage[part, :, 0:128], stage[part, :, 128:256])
                part_out[step * 4 + xt] = chosen.astype(BF)

                def send(xt=xt):
                    pltpu.make_async_remote_copy(
                        src_ref=part_out.at[step * 4 + xt],
                        dst_ref=(relay_in if relayed else part_in).at[step * 4 + x],
                        send_sem=sent_sem.at[0],
                        recv_sem=(relay_sems if relayed else part_sems).at[step],
                        device_id={"vol": xt * 8 + (z if relayed else zt)},
                        device_id_type=MESH,
                    ).start()

                if part == 1 and k == 1:
                    if not relayed:
                        pl.when(step < 7)(send)
                else:
                    send()
        return carry

    def relay(step):
        arrived = relay_in.at[pl.ds(step * 4, 3)]
        pltpu.make_async_copy(arrived, arrived, relay_sems.at[step]).wait()
        relay_in[step * 4 + x] = part_out[step * 4 + x]
        total = relay_in[step * 4].astype(F32)
        for xs in range(1, 4):
            total = total + relay_in[step * 4 + xs].astype(F32)
        relay_out[step] = total.astype(BF)
        pltpu.make_async_remote_copy(
            src_ref=relay_out.at[step],
            dst_ref=part_in.at[step * 4],
            send_sem=sent_sem.at[0],
            recv_sem=part_sems.at[step],
            device_id={"vol": x * 8 + plane_of(step)},
            device_id_type=MESH,
        ).start()

    lay_at(0)
    lax.fori_loop(0, 2, begin_plane, 0)
    pl.semaphore_wait(barrier, len(met))
    swap = pltpu.make_async_remote_copy(
        src_ref=swap_out,
        dst_ref=swap_in,
        send_sem=swap_sems.at[0],
        recv_sem=swap_sems.at[1],
        device_id=at_zc(0, 1),
        device_id_type=MESH,
    )
    swap.start()
    lax.fori_loop(2, 6, begin_plane, 0)
    swap.wait()
    spec[...] = swap_in[...].astype(F32)
    lay_at(256)
    lax.fori_loop(0, 3, lambda step, carry: finish_plane(step, carry, 1, True), 0)
    lax.fori_loop(3, 6, lambda step, carry: finish_plane(step, carry, 1), 0)
    lax.fori_loop(6, 7, lambda step, carry: finish_plane(step, carry, 0), 0)
    relay(0)
    lax.fori_loop(7, 8, lambda step, carry: finish_plane(step, carry, 0), 0)
    relay(1)
    relay(2)
    part_in[28 + x] = part_out[28 + x]

    total = jnp.zeros((32, 128), F32)
    for step in (3, 4, 5, 6, 7, 0, 1, 2):
        tiles = 1 if step < 3 else 4
        arrived = part_in.at[pl.ds(step * 4, tiles if step < 7 else 3)]
        pltpu.make_async_copy(arrived, arrived, part_sems.at[step]).wait()
        for k in range(tiles):
            total = total + part_in[step * 4 + k].astype(F32)
    total = total * scale[...]
    chosen = picks[...]
    upper = total.astype(BF)
    lower = (total - upper.astype(F32)).astype(BF)
    slots = jnp.dot(chosen, upper, preferred_element_type=F32)
    slots = slots + jnp.dot(chosen, lower, preferred_element_type=F32)
    for k in range(32):
        slot_out[k] = slots[4 * k : 4 * k + 4]
    slot_in[y * 4 + x] = slot_out[y * 4 + x]
    for a, b in by_xz:
        pltpu.make_async_remote_copy(
            src_ref=slot_out.at[(y + b) % 8 * 4 + (x + a) % 4],
            dst_ref=slot_in.at[y * 4 + x],
            send_sem=slot_sems.at[0],
            recv_sem=slot_sems.at[1],
            device_id=at_xy(a, b),
            device_id_type=MESH,
        ).start()
    arrived = slot_in.at[pl.ds(0, 31)]
    pltpu.make_async_copy(arrived, arrived, slot_sems.at[1]).wait()
    for xs in range(4):
        chunk = slot_in[xs]
        for ys in range(1, 8):
            chunk = chunk + slot_in[ys * 4 + xs]
        for k in range(2):
            tile[k, 2 * xs : 2 * xs + 2, :] = chunk[2 * k : 2 * k + 2]

    for k in range(2):
        residue = (z - own_begins[k] + NF) % 8
        whole = tile[k]
        for zt in range(8):
            last_out[zt * 2 + k] = jnp.where(residue == zt, 1.0, 0.0) * whole
    last_in[z * 2 + core] = last_out[z * 2 + core]
    for a, b in by_zc:
        pltpu.make_async_remote_copy(
            src_ref=last_out.at[(z + a) % 8 * 2 + (core + b) % 2],
            dst_ref=last_in.at[z * 2 + core],
            send_sem=last_sems.at[0],
            recv_sem=last_sems.at[1],
            device_id=at_zc(a, b),
            device_id_type=MESH,
        ).start()
    arrived = last_in.at[pl.ds(0, 15)]
    pltpu.make_async_copy(arrived, arrived, last_sems.at[1]).wait()
    whole = last_in[0]
    for k in range(1, 16):
        whole = whole + last_in[k]
    out_ref[...] = whole

    sent = part_out.at[pl.ds(0, 31)]
    pltpu.make_async_copy(sent, sent, sent_sem.at[0]).wait()
    sent = slot_out.at[pl.ds(0, 31)]
    pltpu.make_async_copy(sent, sent, slot_sems.at[0]).wait()
    sent = last_out.at[pl.ds(0, 15)]
    pltpu.make_async_copy(sent, sent, last_sems.at[0]).wait()


def per_device(series, send_rows, bin_counts, observer_cells):
    in_vmem = pl.BlockSpec(memory_space=pltpu.VMEM)
    chunks = pl.pallas_call(
        kernel,
        out_shape=jax.ShapeDtypeStruct((8, 128), F32),
        in_specs=[pl.BlockSpec(memory_space=pl.ANY)] * 5,
        out_specs=in_vmem,
        scratch_shapes=[
            pltpu.SMEM((16,), jnp.int32),
            pltpu.VMEM((64, NQ * NT), BF),
            pltpu.VMEM((1, 64), jnp.int32),
            pltpu.VMEM((2, OBS), jnp.int32),
            pltpu.VMEM((2 * NF, NT), BF),
            pltpu.VMEM((1024, 128), F32),
            pltpu.VMEM((1024, 128), BF),
            pltpu.VMEM((1024, 128), BF),
            pltpu.VMEM((3, 128, 128), F32),
            pltpu.VMEM((3, 8, OBS), F32),
            pltpu.VMEM((8, OBS), F32),
            pltpu.VMEM((32, 128, OBS), BF),
            pltpu.VMEM((8, 8, 16, 512), BF),
            pltpu.VMEM((6, 8, 16, OBS), F32),
            pltpu.VMEM((128, 32), BF),
            pltpu.VMEM((32, 128), F32),
            pltpu.VMEM((2, 32, 256), F32),
            pltpu.VMEM((32, 32, 128), BF),
            pltpu.VMEM((32, 32, 128), BF),
            pltpu.VMEM((3, 32, 128), BF),
            pltpu.VMEM((12, 32, 128), BF),
            pltpu.VMEM((32, 4, 128), F32),
            pltpu.VMEM((32, 4, 128), F32),
            pltpu.VMEM((2, 8, 128), F32),
            pltpu.VMEM((16, 8, 128), F32),
            pltpu.VMEM((16, 8, 128), F32),
            pltpu.SemaphoreType.DMA((2,)),
            pltpu.SemaphoreType.DMA((1,)),
            pltpu.SemaphoreType.DMA((8,)),
            pltpu.SemaphoreType.DMA((3,)),
            pltpu.SemaphoreType.DMA((2,)),
            pltpu.SemaphoreType.DMA((2,)),
            pltpu.SemaphoreType.DMA((5,)),
        ],
        compiler_params=pltpu.CompilerParams(
            collective_id=0, has_side_effects=True, vmem_limit_bytes=56 << 20
        ),
    )(
        bin_counts,
        series,
        send_rows.reshape(1, -1),
        observer_cells,
        jnp.asarray(dft_rows()),
    )
    return chunks.reshape(4, 2, 128).transpose(1, 0, 2).reshape(1, 1, 2, OBS)


def solution(mesh):
    placed = (P(("vol", "nar"), None), P("vol", "nar", None), P(), P())
    return jax.shard_map(
        per_device,
        mesh=mesh,
        in_specs=placed,
        out_specs=P("nar", "vol", None, None),
        check_vma=False,
    )
```

time: 41.3 us -> 40.6 us (0.983)
  Pallas kernels: 39.9 us -> 39.2 us
    pallas_call x1, Pallas kernels: 39.9 us -> 39.2 us  [per_device(): pl.pallas_call(kernel, out_shape=jax.ShapeDtypeStruct((8, 128), F32), in_...]
where the time goes in v2:
time: 40.6 us; the launch traced here: 40.4 us
  Pallas kernels  39.2 us (97%)
  local copies, waits for them, and re-layouts  1.28 us (3%)
    pallas_call x1, Pallas kernels, per_device(): pl.pallas_call(kernel, out_shape=jax.ShapeDtypeStruct((8, 128), F32), in_...  39.2 us
    unnamed x1, local copies, waits for them, and re-layouts  1.28 us

profile of v2, /device:TPU:1, one launch (start us, length us, event | category | flops | bytes accessed | tf_op | source)
XLA Modules:
  0.0 40.4 jit_solution(16876984987501302891)
XLA Ops:
  0.0 39.2 %shard_map.55 = f32[8,128]{1,0:T(8,128)} custom-call(s32[16]{0:T(128)} %counts_hbm.1, bf16[64,2048]{1,0:T(8,128)(2,1)} %series_hbm.1, s32[1,64]{1,0:T(1,128)} %bitcast.7, s32[2,512]{1,0:T(2,128)} %cells_hbm.1, bf16[512,512]{1,0:T(8,128)(2,1)} %constant.2.clone.dft_hbm), custom_call_target="tpu_custom_call" | custom-call | tf_op jit(solution)/shard_map/pallas_call | solution.py:437
  39.2 1.3 %copy.8 = f32[1,1,2,512]{3,2,1,0:T(2,128)} copy(f32[1,1,2,512]{3,2,1,0:T(2,128)} %bitcast.6) | data formatting | bytes 8192

commit v3 on v2

--- a/solution.py
+++ b/solution.py
@@ -359,18 +359,17 @@
     swap.wait()
     spec[...] = swap_in[...].astype(F32)
     lay_at(256)
-    lax.fori_loop(0, 3, lambda step, carry: finish_plane(step, carry, 1, True), 0)
-    lax.fori_loop(3, 6, lambda step, carry: finish_plane(step, carry, 1), 0)
+    lax.fori_loop(0, 2, lambda step, carry: finish_plane(step, carry, 1, True), 0)
+    lax.fori_loop(2, 6, lambda step, carry: finish_plane(step, carry, 1), 0)
     lax.fori_loop(6, 7, lambda step, carry: finish_plane(step, carry, 0), 0)
     relay(0)
+    relay(1)
     lax.fori_loop(7, 8, lambda step, carry: finish_plane(step, carry, 0), 0)
-    relay(1)
-    relay(2)
     part_in[28 + x] = part_out[28 + x]
 
     total = jnp.zeros((32, 128), F32)
-    for step in (3, 4, 5, 6, 7, 0, 1, 2):
-        tiles = 1 if step < 3 else 4
+    for step in (2, 3, 4, 5, 6, 7, 0, 1):
+        tiles = 1 if step < 2 else 4
         arrived = part_in.at[pl.ds(step * 4, tiles if step < 7 else 3)]
         pltpu.make_async_copy(arrived, arrived, part_sems.at[step]).wait()
         for k in range(tiles):
@@ -459,8 +458,8 @@
             pltpu.VMEM((2, 32, 256), F32),
             pltpu.VMEM((32, 32, 128), BF),
             pltpu.VMEM((32, 32, 128), BF),
-            pltpu.VMEM((3, 32, 128), BF),
-            pltpu.VMEM((12, 32, 128), BF),
+            pltpu.VMEM((2, 32, 128), BF),
+            pltpu.VMEM((8, 32, 128), BF),
             pltpu.VMEM((32, 4, 128), F32),
             pltpu.VMEM((32, 4, 128), F32),
             pltpu.VMEM((2, 8, 128), F32),
@@ -469,7 +468,7 @@
             pltpu.SemaphoreType.DMA((2,)),
             pltpu.SemaphoreType.DMA((1,)),
             pltpu.SemaphoreType.DMA((8,)),
-            pltpu.SemaphoreType.DMA((3,)),
+            pltpu.SemaphoreType.DMA((2,)),
             pltpu.SemaphoreType.DMA((2,)),
             pltpu.SemaphoreType.DMA((2,)),
             pltpu.SemaphoreType.DMA((5,)),

time: 40.6 us -> 40.5 us (level)
  no operation moved by 1% of the time
where the time goes in v3:
time: 40.5 us; the launch traced here: 40.3 us
  Pallas kernels  39 us (96%)
  local copies, waits for them, and re-layouts  1.28 us (3%)
    pallas_call x1, Pallas kernels, per_device(): pl.pallas_call(kernel, out_shape=jax.ShapeDtypeStruct((8, 128), F32), in_...  39 us
    unnamed x1, local copies, waits for them, and re-layouts  1.28 us

profile of v3, /device:TPU:1, one launch (start us, length us, event | category | flops | bytes accessed | tf_op | source)
XLA Modules:
  0.0 40.3 jit_solution(7082305169094573249)
XLA Ops:
  0.0 39.0 %shard_map.55 = f32[8,128]{1,0:T(8,128)} custom-call(s32[16]{0:T(128)} %counts_hbm.1, bf16[64,2048]{1,0:T(8,128)(2,1)} %series_hbm.1, s32[1,64]{1,0:T(1,128)} %bitcast.7, s32[2,512]{1,0:T(2,128)} %cells_hbm.1, bf16[512,512]{1,0:T(8,128)(2,1)} %constant.2.clone.dft_hbm), custom_call_target="tpu_custom_call" | custom-call | tf_op jit(solution)/shard_map/pallas_call | solution.py:436
  39.0 1.3 %copy.8 = f32[1,1,2,512]{3,2,1,0:T(2,128)} copy(f32[1,1,2,512]{3,2,1,0:T(2,128)} %bitcast.6) | data formatting | bytes 8192

commit v4 on v3

--- a/solution.py
+++ b/solution.py
@@ -286,7 +286,7 @@
         for half in range(2):
             lanes = pl.ds(half * 256, 256)
             for j in range(8):
-                begun[step, j, :, lanes] = products(zt, j, lanes, 0, 1)
+                begun[step - 3, j, :, lanes] = products(zt, j, lanes, 0, 1)
         return carry
 
     def finish_plane(step, carry, first, relayed=False):
@@ -297,7 +297,7 @@
             for j in range(8):
                 sums = products(zt, j, lanes, first, 2)
                 if first:
-                    sums = sums + begun[step, j, :, lanes]
+                    sums = sums + begun[step - 3, j, :, lanes]
                 for sg, k in enumerate((8 + j, 7 - j)):
                     total = sums[8 * sg : 8 * sg + 8] * weight[:, lanes]
                     total = total + pltpu.roll(total, 7, 0)
@@ -344,7 +344,7 @@
         ).start()
 
     lay_at(0)
-    lax.fori_loop(0, 2, begin_plane, 0)
+    lax.fori_loop(3, 5, begin_plane, 0)
     pl.semaphore_wait(barrier, len(met))
     swap = pltpu.make_async_remote_copy(
         src_ref=swap_out,
@@ -355,16 +355,17 @@
         device_id_type=MESH,
     )
     swap.start()
-    lax.fori_loop(2, 6, begin_plane, 0)
+    lax.fori_loop(5, 8, begin_plane, 0)
     swap.wait()
     spec[...] = swap_in[...].astype(F32)
     lay_at(256)
-    lax.fori_loop(0, 2, lambda step, carry: finish_plane(step, carry, 1, True), 0)
-    lax.fori_loop(2, 6, lambda step, carry: finish_plane(step, carry, 1), 0)
-    lax.fori_loop(6, 7, lambda step, carry: finish_plane(step, carry, 0), 0)
+    lax.fori_loop(0, 2, lambda step, carry: finish_plane(step, carry, 0, True), 0)
+    lax.fori_loop(2, 3, lambda step, carry: finish_plane(step, carry, 0), 0)
+    lax.fori_loop(3, 6, lambda step, carry: finish_plane(step, carry, 1), 0)
+    lax.fori_loop(6, 7, lambda step, carry: finish_plane(step, carry, 1), 0)
     relay(0)
     relay(1)
-    lax.fori_loop(7, 8, lambda step, carry: finish_plane(step, carry, 0), 0)
+    lax.fori_loop(7, 8, lambda step, carry: finish_plane(step, carry, 1), 0)
     part_in[28 + x] = part_out[28 + x]
 
     total = jnp.zeros((32, 128), F32)
@@ -452,7 +453,7 @@
             pltpu.VMEM((8, OBS), F32),
             pltpu.VMEM((32, 128, OBS), BF),
             pltpu.VMEM((8, 8, 16, 512), BF),
-            pltpu.VMEM((6, 8, 16, OBS), F32),
+            pltpu.VMEM((5, 8, 16, OBS), F32),
             pltpu.VMEM((128, 32), BF),
             pltpu.VMEM((32, 128), F32),
             pltpu.VMEM((2, 32, 256), F32),

time: 40.5 us -> 41.1 us (1.015)
  Pallas kernels: 39 us -> 39.7 us
    pallas_call x1, Pallas kernels: 39 us -> 39.7 us  [per_device(): pl.pallas_call(kernel, out_shape=jax.ShapeDtypeStruct((8, 128), F32), in_...]
where the time goes in v4:
time: 41.1 us; the launch traced here: 41 us
  Pallas kernels  39.7 us (97%)
  local copies, waits for them, and re-layouts  1.28 us (3%)
    pallas_call x1, Pallas kernels, per_device(): pl.pallas_call(kernel, out_shape=jax.ShapeDtypeStruct((8, 128), F32), in_...  39.7 us
    unnamed x1, local copies, waits for them, and re-layouts  1.28 us

profile of v4, /device:TPU:1, one launch (start us, length us, event | category | flops | bytes accessed | tf_op | source)
XLA Modules:
  0.0 41.0 jit_solution(15476954454319627794)
XLA Ops:
  0.0 39.7 %shard_map.55 = f32[8,128]{1,0:T(8,128)} custom-call(s32[16]{0:T(128)} %counts_hbm.1, bf16[64,2048]{1,0:T(8,128)(2,1)} %series_hbm.1, s32[1,64]{1,0:T(1,128)} %bitcast.7, s32[2,512]{1,0:T(2,128)} %cells_hbm.1, bf16[512,512]{1,0:T(8,128)(2,1)} %constant.2.clone.dft_hbm), custom_call_target="tpu_custom_call" | custom-call | tf_op jit(solution)/shard_map/pallas_call | solution.py:437
  39.7 1.3 %copy.8 = f32[1,1,2,512]{3,2,1,0:T(2,128)} copy(f32[1,1,2,512]{3,2,1,0:T(2,128)} %bitcast.6) | data formatting | bytes 8192
